TPU v7x, 32 devices: a whole 2x2x4 slice. The times are simulated.
32 devices in a mesh: leaf: 8 (over z, y), rep: 4 (over x, core).
Axes of the slice: x: 2, y: 2, z: 4, core: 2. Of those that a mesh axis runs over, the one named last changes fastest.
Arguments:
- fine_moments: bfloat16 [128, 8, 8, 152], P('leaf'), may hold values from -6 to 6
- fine_present: int32 [128, 8, 8], P('leaf'), may hold values 0 or 1
- coarse_moments: bfloat16 [64, 4, 4, 152], P('leaf'), may hold values from -6 to 6
- coarse_present: int32 [64, 4, 4], P('leaf'), may hold values 0 or 1
- coarse_incoming: float32 [64, 4, 4, 152], P('leaf'), may hold values from -6 to 6
- check_to_density: float32 [152, 152], replicated, may hold values from -0.5 to 0.5
Outputs:
- fine_density: float32 [8, 64, 4, 4, 152], P('rep', 'leaf')
All inputs are finite; a program needn't handle non-finite values. No bound on the sum of `fine_present` or of `coarse_present` on one device may be relied on, other than what follows from the above.
Results may differ from a plain program's by a relative error of at most 0.0003.
The roundings to bfloat16 on the way count: a program that leaves them out, or rounds other values in their place, can miss the bound.
Values may be sent and summed in bfloat16 or wider, within the bound.
A program may use at most 64 MiB of HBM per device.

v0:
```python
import jax
import jax.numpy as jnp
import numpy as np
from jax import lax
from jax.sharding import PartitionSpec as P

ORDER = 6


strength = 0.04
group_size = 24


def padded_2(shard, sides, width):
    for axis, dim in sides:
        size, length = (lax.axis_size(axis), shard.shape[dim])
        up = [(i, (i + 1) % size) for i in range(size - 1)]
        down = [(j, i) for i, j in up]
        last = lax.slice_in_dim(shard, length - width, length, axis=dim)
        first = lax.slice_in_dim(shard, 0, width, axis=dim)
        before = lax.ppermute(last, axis, up)
        after = lax.ppermute(first, axis, down)
        shard = jnp.concatenate([before, shard, after], axis=dim)
    return shard


def surface_points(order):
    chosen = []
    for height in range(order):
        for across in range(order):
            for along in range(order):
                on_edge = [coordinate in (0, order - 1) for coordinate in (height, across, along)]
                if any(on_edge):
                    chosen.append((height, across, along))
    return np.array(chosen, np.int32)


def surface_coordinates():
    lattice = jnp.asarray(surface_points(ORDER), jnp.int32).astype(jnp.float32)
    return lattice * (2.0 / (ORDER - 1)) - 1.0


def octant_bit_table():
    return np.array(
        [[octant >> 2 & 1, octant >> 1 & 1, octant & 1] for octant in range(8)], np.int32
    )


def interaction_table():
    entries = np.zeros((8, 192, 4), np.int32)
    entries[:, :, :3] = 3
    for octant in range(8):
        parity = octant_bit_table()[octant]
        found = []
        for vertical in range(-2 - parity[0], 4 - parity[0]):
            for lateral in range(-2 - parity[1], 4 - parity[1]):
                for forward in range(-2 - parity[2], 4 - parity[2]):
                    if max(abs(vertical), abs(lateral), abs(forward)) >= 2:
                        found.append((vertical, lateral, forward))
        entries[octant, : len(found), :3] = np.array(found, np.int32)
        entries[octant, : len(found), 3] = 1
    return entries


def translation_ops(offsets, valid):
    surface = surface_coordinates()
    gaps = []
    for axis_index in range(3):
        target = 0.525 * surface[:, axis_index]
        source = (
            0.525 * surface[None, :, axis_index]
            + offsets[:, axis_index].astype(jnp.float32)[:, None]
        )
        gaps.append(target[None, None, :] - source[:, :, None])
    squared = gaps[0] ** 2 + gaps[1] ** 2 + gaps[2] ** 2
    return (strength * valid[:, None, None] / jnp.sqrt(squared)).astype(jnp.bfloat16)


def transfer_ops(octant_bits):
    surface = surface_coordinates()
    gaps = []
    for axis_index in range(3):
        child = (
            octant_bits[:, axis_index].astype(jnp.float32)[:, None]
            - 0.5
            + 0.525 * surface[None, :, axis_index]
        )
        parent = 2.95 * surface[:, axis_index]
        gaps.append(child[:, None, :] - parent[None, :, None])
    squared = gaps[0] ** 2 + gaps[1] ** 2 + gaps[2] ** 2
    return (strength / jnp.sqrt(squared)).astype(jnp.bfloat16)


def parity_stack(padded):
    dims = padded.shape
    shaped = padded.reshape(dims[0] // 2, 2, dims[1] // 2, 2, dims[2] // 2, 2, dims[3])
    return shaped.transpose(1, 3, 5, 0, 2, 4, 6).reshape(
        8, dims[0] // 2, dims[1] // 2, dims[2] // 2, dims[3]
    )


def strided_cut(stacked, corner, extent):
    parity = corner % 2
    selected = parity[0] * 4 + parity[1] * 2 + parity[2]
    starts = corner // 2
    nought = jnp.zeros((), jnp.int32)
    window = lax.dynamic_slice(
        stacked,
        (selected, starts[0], starts[1], starts[2], nought),
        (1, extent[0] // 2, extent[1] // 2, extent[2] // 2, stacked.shape[4]),
    )
    return window.reshape(-1, stacked.shape[4])


def octant_layout(field):
    halves = (field.shape[0] // 2, field.shape[1] // 2, field.shape[2] // 2)
    trailing = field.shape[3:]
    shaped = field.reshape((halves[0], 2, halves[1], 2, halves[2], 2) + trailing)
    moved = shaped.transpose((1, 3, 5, 0, 2, 4) + tuple(range(6, 6 + len(trailing))))
    return moved.reshape((8, halves[0] * halves[1] * halves[2]) + trailing)


def natural_layout(grouped, extent):
    feature = grouped.shape[2]
    shaped = grouped.reshape(2, 2, 2, extent[0] // 2, extent[1] // 2, extent[2] // 2, feature)
    return shaped.transpose(3, 0, 4, 1, 5, 2, 6).reshape(extent[0], extent[1], extent[2], feature)


def density(check, check_to_density, present_rows, factor):
    mapped = jnp.einsum(
        "nrk,kl->nrl",
        check,
        check_to_density,
        precision=lax.Precision.HIGHEST,
        preferred_element_type=jnp.float32,
    )
    return factor * mapped * present_rows[..., None]


def pad_plane(field):
    return jnp.pad(field, ((0, 0), (3, 3), (3, 3), (0, 0)))


def bits_of(octant):
    return jnp.stack([octant // 4, octant // 2 % 2, octant % 2])


def octant_terms(fine_stack, coarse_stack, octant_bits, entries, fine_extent, coarse_extent):
    feature = fine_stack.shape[4]
    fine_count = fine_extent[0] * fine_extent[1] * fine_extent[2] // 8
    coarse_count = coarse_extent[0] * coarse_extent[1] * coarse_extent[2] // 8

    def turn(carried, batch):
        corners = octant_bits[None, :] + batch[:, :3] + 3

        def fine_cut(corner):
            return strided_cut(fine_stack, corner, fine_extent)

        def coarse_cut(corner):
            return strided_cut(coarse_stack, corner, coarse_extent)

        weights = translation_ops(batch[:, :3], batch[:, 3].astype(jnp.float32))
        fine_sources = jax.vmap(fine_cut)(corners)
        coarse_sources = jax.vmap(coarse_cut)(corners)
        fine_running = carried[0] + jnp.einsum(
            "grk,gkl->rl", fine_sources, weights, preferred_element_type=jnp.float32
        )
        coarse_running = carried[1] + jnp.einsum(
            "grk,gkl->rl", coarse_sources, weights * 0.5, preferred_element_type=jnp.float32
        )
        return ((fine_running, coarse_running), None)

    initial = (
        jnp.zeros((fine_count, feature), jnp.float32),
        jnp.zeros((coarse_count, feature), jnp.float32),
    )
    carried, _ = lax.scan(turn, initial, entries.reshape(-1, group_size, 4))
    return carried


def shards(
    fine_moments, fine_present, coarse_moments, coarse_present, coarse_incoming, check_to_density
):
    feature = fine_moments.shape[3]
    fine_extent = fine_moments.shape[:3]
    coarse_extent = coarse_moments.shape[:3]
    fine_masked = fine_moments * fine_present[..., None].astype(jnp.bfloat16)
    coarse_masked = coarse_moments * coarse_present[..., None].astype(jnp.bfloat16)
    fine_rim = padded_2(fine_masked, (("leaf", 0),), 3)
    coarse_rim = padded_2(coarse_masked, (("leaf", 0),), 3)
    fine_stack = parity_stack(pad_plane(fine_rim))
    coarse_stack = parity_stack(pad_plane(coarse_rim))
    offsets_table = jnp.asarray(interaction_table())
    replica = lax.axis_index("rep")
    groups = lax.axis_size("rep")
    mine = 8 // groups
    first = replica * mine
    coarse_inflow = octant_layout(coarse_incoming)
    coarse_mask = octant_layout(coarse_present).astype(jnp.float32)
    fine_mask = octant_layout(fine_present).astype(jnp.float32)
    share = offsets_table.shape[1] // groups
    fine_parts = []
    coarse_parts = []
    for octant in range(8):
        entries = lax.dynamic_slice_in_dim(offsets_table[octant], replica * share, share, 0)
        fine_part, coarse_part = octant_terms(
            fine_stack,
            coarse_stack,
            bits_of(jnp.int32(octant)),
            entries,
            fine_extent,
            coarse_extent,
        )
        fine_parts.append(fine_part)
        coarse_parts.append(coarse_part)
    coarse_check = lax.psum(jnp.stack(coarse_parts), "rep") + coarse_inflow
    coarse_density = density(coarse_check, check_to_density, coarse_mask, 2.0).astype(jnp.bfloat16)
    fine_check = lax.psum_scatter(jnp.stack(fine_parts), "rep", scatter_dimension=0, tiled=True)
    parents = natural_layout(coarse_density, coarse_extent).reshape(-1, feature)
    own_bits = jnp.stack([bits_of(first + slot_index) for slot_index in range(mine)])
    fine_check = fine_check + jnp.einsum(
        "rk,nkl->nrl", parents, transfer_ops(own_bits), preferred_element_type=jnp.float32
    )
    own_fine_mask = lax.dynamic_slice_in_dim(fine_mask, first, mine, 0)
    fine_density = density(fine_check, check_to_density, own_fine_mask, 1.0)
    return fine_density.reshape(
        mine, fine_extent[0] // 2, fine_extent[1] // 2, fine_extent[2] // 2, feature
    )


def solution(mesh):
    in_specs = (
        P("leaf", None, None, None),
        P("leaf", None, None),
        P("leaf", None, None, None),
        P("leaf", None, None),
        P("leaf", None, None, None),
        P(),
    )
    out_specs = P("rep", "leaf", None, None, None)
    return jax.shard_map(shards, mesh=mesh, in_specs=in_specs, out_specs=out_specs, check_vma=False)
```

profile of v0, /device:TPU:0, one launch (start us, length us, event | category | flops | bytes accessed | tf_op | source)
XLA Modules:
  0.0 428.9 jit_solution(9477055768931645481)
XLA Ops:
  8.8 4.9 %collective-permute-start = (bf16[3,8,8,152]{3,2,1,0:T(8,128)(2,1)S(1)}, bf16[3,8,8,152]{3,2,1,0:T(8,128)(2,1)S(1)}, u32[]{:S(2)}, u32[]{:S(2)}) collective-permute-start(bf16[3,8,8,152]{3,2,1,0:T(8,128)(2,1)S(1)} %get-tuple-element.1664), channel_id=1, source_target_pairs={{0,4},{4,8},{8,12},{12,16},{16,20},{20,24},{24,28},{1,5},{5,9},{9,... | collective-permute-start | bytes 175112 | tf_op jit(solution)/shard_map/ppermute | solution.py:21
  16.7 4.5 %collective-permute-start.2 = (bf16[3,4,4,152]{3,2,1,0:T(4,128)(2,1)S(1)}, bf16[3,4,4,152]{3,2,1,0:T(4,128)(2,1)S(1)}, u32[]{:S(2)}, u32[]{:S(2)}) collective-permute-start(bf16[3,4,4,152]{3,2,1,0:T(4,128)(2,1)S(1)} %get-tuple-element.1666), channel_id=1, source_target_pairs={{0,4},{4,8},{8,12},{12,16},{16,20},{20,24},{24,28},{1,5},{5,9},{9,... | collective-permute-start | bytes 43784 | tf_op jit(solution)/shard_map/ppermute | solution.py:21
  41.8 4.8 %reshape.1980 = bf16[11,2,7,2,7,2,152]{6,5,4,3,2,1,0:T(2,128)(2,1)S(1)} reshape(bf16[22,14,14,152]{3,2,1,0:T(8,128)(2,1)} %select_maximum_fusion) | data formatting | bytes 2621696 | tf_op jit(solution)/shard_map/reshape | solution.py:96
  49.5 4.8 %reshape.1691 = bf16[8,11,7,7,152]{4,0,3,2,1:T(8,128)(2,1)S(1)} reshape(bf16[2,2,2,11,7,7,152]{6,2,1,0,5,4,3:T(2,128)(2,1)} %copy.119) | data formatting | bytes 2621696 | tf_op jit(solution)/shard_map/reshape | solution.py:97
  54.3 37.3 %while.129 = (s32[]{:T(128)}, f32[128,152]{0,1:T(8,128)}, f32[16,152]{1,0:T(8,128)}, s32[2,24,4]{1,0,2:T(2,128)S(1)}, bf16[8,11,7,7,152]{4,0,3,2,1:T(8,128)(2,1)...) while((s32[]{:T(128)}, f32[128,152]{0,1:T(8,128)}, ...), condition=%wide.region_3.4_spmd.clone.clone, body=%wide.region_2.3_spmd.clone.clone.sunk | while | flops 173061552 | bytes 3476288 | solution.py:177
  54.8 8.0 %gather_fusion.2 = bf16[24,8,4,4,152]{4,0,3,2,1:T(8,128)(2,1)} fusion(bf16[8,11,7,7,152]{4,0,3,2,1:T(8,128)(2,1)S(1)} %get-tuple-element.2219, s32[24]{0:T(128)S(1)} %fusion.463), kind=kCustom, calls=%fused_computation.2.clone.clone.clone.1 | custom fusion | bytes 1868256 | tf_op jit(solution)/shard_map/while/body/eval_jaxpr/vmap()/gather | solution.py:107
  62.8 5.1 %fusion.464 = f32[128,152]{0,1:T(8,128)} fusion(bf16[24,128,152]{2,0,1:T(8,128)(2,1)} %bitcast.509, f32[24,152]{1,0:T(8,128)S(1)} %get-tuple-element.2055, f32[152]{0:T(256)S(1)} %bitcast.560, f32[24,152]{1,0:T(8,128)S(1)} %get-tuple-element.2056, f32[152]{0:T(256)S(1)} %bitcast.563, f32[24,152]{1,0:T(8,128)S(1)} %broadcast_add_fusion.46, ...), kind=kOutput, calls=%fused_computation.92.clone.1 | convolution fusion | flops 147534848 | bytes 1135233 | tf_op jit(solution)/shard_map/while/body/eval_jaxpr/grk,gkl->rl/dot_general | solution.py:165
  73.0 8.0 %gather_fusion.2 = bf16[24,8,4,4,152]{4,0,3,2,1:T(8,128)(2,1)} fusion(bf16[8,11,7,7,152]{4,0,3,2,1:T(8,128)(2,1)S(1)} %get-tuple-element.2219, s32[24]{0:T(128)S(1)} %fusion.463), kind=kCustom, calls=%fused_computation.2.clone.clone.clone.1 | custom fusion | bytes 1868256 | tf_op jit(solution)/shard_map/while/body/eval_jaxpr/vmap()/gather | solution.py:107
  81.0 5.1 %fusion.464 = f32[128,152]{0,1:T(8,128)} fusion(bf16[24,128,152]{2,0,1:T(8,128)(2,1)} %bitcast.509, f32[24,152]{1,0:T(8,128)S(1)} %get-tuple-element.2055, f32[152]{0:T(256)S(1)} %bitcast.560, f32[24,152]{1,0:T(8,128)S(1)} %get-tuple-element.2056, f32[152]{0:T(256)S(1)} %bitcast.563, f32[24,152]{1,0:T(8,128)S(1)} %broadcast_add_fusion.46, ...), kind=kOutput, calls=%fused_computation.92.clone.1 | convolution fusion | flops 147534848 | bytes 1135233 | tf_op jit(solution)/shard_map/while/body/eval_jaxpr/grk,gkl->rl/dot_general | solution.py:165
  91.6 35.5 %while.128 = (s32[]{:T(128)}, f32[128,152]{0,1:T(8,128)S(1)}, f32[16,152]{1,0:T(8,128)}, s32[2,24,4]{1,0,2:T(2,128)S(1)}, bf16[8,11,7,7,152]{4,0,3,2,1:T(8,128)(...) while((s32[]{:T(128)}, f32[128,152]{0,1:T(8,128)S(1)}, ...), condition=%wide.region_1.2_spmd.clone.clone, body=%wide.region_0.1_spmd.clone.clone.sunk | while | flops 173061488 | bytes 3554148 | solution.py:177
  92.2 8.0 %gather_fusion = bf16[24,8,4,4,152]{4,0,3,2,1:T(8,128)(2,1)} fusion(bf16[8,11,7,7,152]{4,0,3,2,1:T(8,128)(2,1)S(1)} %get-tuple-element.2190, s32[24]{0:T(128)S(1)} %fusion.456), kind=kCustom, calls=%fused_computation.clone.clone.clone.1 | custom fusion | bytes 1868256 | tf_op jit(solution)/shard_map/while/body/eval_jaxpr/vmap()/gather | solution.py:107
  109.8 8.0 %gather_fusion = bf16[24,8,4,4,152]{4,0,3,2,1:T(8,128)(2,1)} fusion(bf16[8,11,7,7,152]{4,0,3,2,1:T(8,128)(2,1)S(1)} %get-tuple-element.2190, s32[24]{0:T(128)S(1)} %fusion.456), kind=kCustom, calls=%fused_computation.clone.clone.clone.1 | custom fusion | bytes 1868256 | tf_op jit(solution)/shard_map/while/body/eval_jaxpr/vmap()/gather | solution.py:107
  128.5 37.4 %while.130 = (s32[]{:T(128)}, f32[128,152]{0,1:T(8,128)S(1)}, f32[16,152]{1,0:T(8,128)}, s32[2,24,4]{1,0,2:T(2,128)S(1)}, bf16[8,11,7,7,152]{4,0,3,2,1:T(8,128)(...) while((s32[]{:T(128)}, f32[128,152]{0,1:T(8,128)S(1)}, ...), condition=%wide.region_5.6_spmd.clone.clone, body=%wide.region_4.5_spmd.clone.clone.sunk | while | flops 173061552 | bytes 3476288 | solution.py:177
  129.6 8.0 %gather_fusion.4 = bf16[24,8,4,4,152]{4,0,3,2,1:T(8,128)(2,1)} fusion(bf16[8,11,7,7,152]{4,0,3,2,1:T(8,128)(2,1)S(1)} %get-tuple-element.2249, s32[24]{0:T(128)S(1)} %fusion.470), kind=kCustom, calls=%fused_computation.4.clone.clone.clone.1 | custom fusion | bytes 1868256 | tf_op jit(solution)/shard_map/while/body/eval_jaxpr/vmap()/gather | solution.py:107
  147.8 8.0 %gather_fusion.4 = bf16[24,8,4,4,152]{4,0,3,2,1:T(8,128)(2,1)} fusion(bf16[8,11,7,7,152]{4,0,3,2,1:T(8,128)(2,1)S(1)} %get-tuple-element.2249, s32[24]{0:T(128)S(1)} %fusion.470), kind=kCustom, calls=%fused_computation.4.clone.clone.clone.1 | custom fusion | bytes 1868256 | tf_op jit(solution)/shard_map/while/body/eval_jaxpr/vmap()/gather | solution.py:107
  166.5 35.6 %while.131 = (s32[]{:T(128)}, f32[128,152]{0,1:T(8,128)S(1)}, f32[16,152]{1,0:T(8,128)S(1)}, s32[2,24,4]{1,0,2:T(2,128)S(1)}, bf16[8,11,7,7,152]{4,0,3,2,1:T(8,1...) while((s32[]{:T(128)}, f32[128,152]{0,1:T(8,128)S(1)}, ...), condition=%wide.region_7.8_spmd.clone.clone, body=%wide.region_6.7_spmd.clone.clone.sunk | while | flops 173061552 | bytes 3476288 | solution.py:177
  167.7 8.0 %gather_fusion.6 = bf16[24,8,4,4,152]{4,0,3,2,1:T(8,128)(2,1)} fusion(bf16[8,11,7,7,152]{4,0,3,2,1:T(8,128)(2,1)S(1)} %get-tuple-element.2279, s32[24]{0:T(128)S(1)} %fusion.477), kind=kCustom, calls=%fused_computation.6.clone.clone.clone.1 | custom fusion | bytes 1868256 | tf_op jit(solution)/shard_map/while/body/eval_jaxpr/vmap()/gather | solution.py:107
  185.3 8.0 %gather_fusion.6 = bf16[24,8,4,4,152]{4,0,3,2,1:T(8,128)(2,1)} fusion(bf16[8,11,7,7,152]{4,0,3,2,1:T(8,128)(2,1)S(1)} %get-tuple-element.2279, s32[24]{0:T(128)S(1)} %fusion.477), kind=kCustom, calls=%fused_computation.6.clone.clone.clone.1 | custom fusion | bytes 1868256 | tf_op jit(solution)/shard_map/while/body/eval_jaxpr/vmap()/gather | solution.py:107
  203.4 37.6 %while.132 = (s32[]{:T(128)}, f32[128,152]{0,1:T(8,128)S(1)}, f32[16,152]{1,0:T(8,128)}, s32[2,24,4]{1,0,2:T(2,128)S(1)}, bf16[8,11,7,7,152]{4,0,3,2,1:T(8,128)(...) while((s32[]{:T(128)}, f32[128,152]{0,1:T(8,128)S(1)}, ...), condition=%wide.region_9.10_spmd.clone.clone, body=%wide.region_8.9_spmd.clone.clone.sunk | while | flops 173061552 | bytes 3476288 | solution.py:177
  204.7 8.0 %gather_fusion.8 = bf16[24,8,4,4,152]{4,0,3,2,1:T(8,128)(2,1)} fusion(bf16[8,11,7,7,152]{4,0,3,2,1:T(8,128)(2,1)S(1)} %get-tuple-element.2309, s32[24]{0:T(128)S(1)} %fusion.484), kind=kCustom, calls=%fused_computation.8.clone.clone.clone.1 | custom fusion | bytes 1868256 | tf_op jit(solution)/shard_map/while/body/eval_jaxpr/vmap()/gather | solution.py:107
  222.9 8.0 %gather_fusion.8 = bf16[24,8,4,4,152]{4,0,3,2,1:T(8,128)(2,1)} fusion(bf16[8,11,7,7,152]{4,0,3,2,1:T(8,128)(2,1)S(1)} %get-tuple-element.2309, s32[24]{0:T(128)S(1)} %fusion.484), kind=kCustom, calls=%fused_computation.8.clone.clone.clone.1 | custom fusion | bytes 1868256 | tf_op jit(solution)/shard_map/while/body/eval_jaxpr/vmap()/gather | solution.py:107
  241.6 35.5 %while.133 = (s32[]{:T(128)}, f32[128,152]{0,1:T(8,128)S(1)}, f32[16,152]{1,0:T(8,128)S(1)}, s32[2,24,4]{1,0,2:T(2,128)S(1)}, bf16[8,11,7,7,152]{4,0,3,2,1:T(8,1...) while((s32[]{:T(128)}, f32[128,152]{0,1:T(8,128)S(1)}, ...), condition=%wide.region_11.12_spmd.clone.clone, body=%wide.region_10.11_spmd.clone.clone.sunk | while | flops 173061552 | bytes 3476288 | solution.py:177
  242.7 8.0 %gather_fusion.10 = bf16[24,8,4,4,152]{4,0,3,2,1:T(8,128)(2,1)} fusion(bf16[8,11,7,7,152]{4,0,3,2,1:T(8,128)(2,1)S(1)} %get-tuple-element.2339, s32[24]{0:T(128)S(1)} %fusion.491), kind=kCustom, calls=%fused_computation.10.clone.clone.clone.1 | custom fusion | bytes 1868256 | tf_op jit(solution)/shard_map/while/body/eval_jaxpr/vmap()/gather | solution.py:107
  260.4 8.0 %gather_fusion.10 = bf16[24,8,4,4,152]{4,0,3,2,1:T(8,128)(2,1)} fusion(bf16[8,11,7,7,152]{4,0,3,2,1:T(8,128)(2,1)S(1)} %get-tuple-element.2339, s32[24]{0:T(128)S(1)} %fusion.491), kind=kCustom, calls=%fused_computation.10.clone.clone.clone.1 | custom fusion | bytes 1868256 | tf_op jit(solution)/shard_map/while/body/eval_jaxpr/vmap()/gather | solution.py:107
  278.4 36.7 %while.134 = (s32[]{:T(128)}, f32[128,152]{0,1:T(8,128)S(1)}, f32[16,152]{1,0:T(8,128)}, s32[2,24,4]{1,0,2:T(2,128)S(1)}, bf16[8,11,7,7,152]{4,0,3,2,1:T(8,128)(...) while((s32[]{:T(128)}, f32[128,152]{0,1:T(8,128)S(1)}, ...), condition=%wide.region_13.14_spmd.clone.clone, body=%wide.region_12.13_spmd.clone.clone.sunk | while | flops 173061552 | bytes 3554168 | solution.py:177
  279.5 8.0 %gather_fusion.12 = bf16[24,8,4,4,152]{4,0,3,2,1:T(8,128)(2,1)} fusion(bf16[8,11,7,7,152]{4,0,3,2,1:T(8,128)(2,1)S(1)} %get-tuple-element.2369, s32[24]{0:T(128)S(1)} %fusion.498), kind=kCustom, calls=%fused_computation.12.clone.clone.clone.1 | custom fusion | bytes 1868256 | tf_op jit(solution)/shard_map/while/body/eval_jaxpr/vmap()/gather | solution.py:107
  297.8 8.0 %gather_fusion.12 = bf16[24,8,4,4,152]{4,0,3,2,1:T(8,128)(2,1)} fusion(bf16[8,11,7,7,152]{4,0,3,2,1:T(8,128)(2,1)S(1)} %get-tuple-element.2369, s32[24]{0:T(128)S(1)} %fusion.498), kind=kCustom, calls=%fused_computation.12.clone.clone.clone.1 | custom fusion | bytes 1868256 | tf_op jit(solution)/shard_map/while/body/eval_jaxpr/vmap()/gather | solution.py:107
  315.8 35.5 %while.135 = (s32[]{:T(128)}, f32[128,152]{0,1:T(8,128)}, f32[16,152]{1,0:T(8,128)S(1)}, s32[2,24,4]{1,0,2:T(2,128)S(1)}, bf16[8,11,7,7,152]{4,0,3,2,1:T(8,128)(...) while((s32[]{:T(128)}, f32[128,152]{0,1:T(8,128)}, ...), condition=%wide.region_15.16_spmd.clone.clone, body=%wide.region_14.15_spmd.clone.clone.sunk | while | flops 173061552 | bytes 4098916 | solution.py:177
  316.3 8.0 %gather_fusion.14 = bf16[24,8,4,4,152]{4,0,3,2,1:T(8,128)(2,1)} fusion(bf16[8,11,7,7,152]{4,0,3,2,1:T(8,128)(2,1)S(1)} %get-tuple-element.2397, s32[24]{0:T(128)S(1)} %fusion.505), kind=kCustom, calls=%fused_computation.14.clone.clone.clone.1 | custom fusion | bytes 1868256 | tf_op jit(solution)/shard_map/while/body/eval_jaxpr/vmap()/gather | solution.py:107
  333.9 8.0 %gather_fusion.14 = bf16[24,8,4,4,152]{4,0,3,2,1:T(8,128)(2,1)} fusion(bf16[8,11,7,7,152]{4,0,3,2,1:T(8,128)(2,1)S(1)} %get-tuple-element.2397, s32[24]{0:T(128)S(1)} %fusion.505), kind=kCustom, calls=%fused_computation.14.clone.clone.clone.1 | custom fusion | bytes 1868256 | tf_op jit(solution)/shard_map/while/body/eval_jaxpr/vmap()/gather | solution.py:107
  370.4 23.6 %all-reduce.4.cloned.1.call-done = f32[8,16,152]{2,1,0:T(8,128)} async-done(((f32[8,16,152]{2,1,0:T(8,128)}), f32[8,16,152]{2,1,0:T(8,128)}) %all-reduce.4.cloned.1.call-update) | async-done | bytes 77840 | tf_op jit(solution)/shard_map/psum | solution.py:216
  395.3 23.6 %reduce-scatter.2.cloned.1.call-done = f32[2,128,152]{1,2,0:T(8,128)} async-done(((f32[8,128,152]{1,2,0:T(8,128)}), f32[2,128,152]{1,2,0:T(8,128)}) %reduce-scatter.2.cloned.1.call-update) | async-done | bytes 155664 | tf_op jit(solution)/shard_map/reduce_scatter | solution.py:218
  (387 shorter events, 207.8 us)
Async XLA Ops:
  6.5 387.4 %copy-start = (f32[152,152]{1,0:T(8,128)S(1)}, f32[152,152]{1,0:T(8,128)}, u32[]{:S(2)}) copy-start(f32[152,152]{1,0:T(8,128)} %param.37) | copy-start | bytes 277252
  6.5 387.4 %all-reduce.4.cloned.1.call-start = ((), (), s32[]{:S(2)}) async-start(), calls=%async_computation.2 | async-start | bytes 262144 | tf_op jit(solution)/shard_map/psum | solution.py:216
  8.8 31.2 %collective-permute-start = (bf16[3,8,8,152]{3,2,1,0:T(8,128)(2,1)S(1)}, bf16[3,8,8,152]{3,2,1,0:T(8,128)(2,1)S(1)}, u32[]{:S(2)}, u32[]{:S(2)}) collective-permute-start(bf16[3,8,8,152]{3,2,1,0:T(8,128)(2,1)S(1)} %get-tuple-element.1664), channel_id=1, source_target_pairs={{0,4},{4,8},{8,12},{12,16},{16,20},{20,24},{24,28},{1,5},{5,9},{9,... | collective-permute-start | bytes 175112 | tf_op jit(solution)/shard_map/ppermute | solution.py:21
  13.6 26.3 %collective-permute-start.1 = (bf16[3,8,8,152]{3,2,1,0:T(8,128)(2,1)S(1)}, bf16[3,8,8,152]{3,2,1,0:T(8,128)(2,1)S(1)}, u32[]{:S(2)}, u32[]{:S(2)}) collective-permute-start(bf16[3,8,8,152]{3,2,1,0:T(8,128)(2,1)S(1)} %get-tuple-element.1665), channel_id=1, source_target_pairs={{4,0},{8,4},{12,8},{16,12},{20,16},{24,20},{28,24},{5,1},{9,5},{13... | collective-permute-start | bytes 175112 | tf_op jit(solution)/shard_map/ppermute | solution.py:22
  16.7 18.8 %collective-permute-start.2 = (bf16[3,4,4,152]{3,2,1,0:T(4,128)(2,1)S(1)}, bf16[3,4,4,152]{3,2,1,0:T(4,128)(2,1)S(1)}, u32[]{:S(2)}, u32[]{:S(2)}) collective-permute-start(bf16[3,4,4,152]{3,2,1,0:T(4,128)(2,1)S(1)} %get-tuple-element.1666), channel_id=1, source_target_pairs={{0,4},{4,8},{8,12},{12,16},{16,20},{20,24},{24,28},{1,5},{5,9},{9,... | collective-permute-start | bytes 43784 | tf_op jit(solution)/shard_map/ppermute | solution.py:21
  21.3 14.3 %collective-permute-start.3 = (bf16[3,4,4,152]{3,2,1,0:T(4,128)(2,1)S(1)}, bf16[3,4,4,152]{3,2,1,0:T(4,128)(2,1)S(1)}, u32[]{:S(2)}, u32[]{:S(2)}) collective-permute-start(bf16[3,4,4,152]{3,2,1,0:T(4,128)(2,1)S(1)} %get-tuple-element.1667), channel_id=1, source_target_pairs={{4,0},{8,4},{12,8},{16,12},{20,16},{24,20},{28,24},{5,1},{9,5},{13... | collective-permute-start | bytes 43784 | tf_op jit(solution)/shard_map/ppermute | solution.py:22
  100.2 6.0 %copy-start.30 = (f32[16,152]{1,0:T(8,128)S(1)}, f32[16,152]{1,0:T(8,128)}, u32[]{:S(2)}) copy-start(f32[16,152]{1,0:T(8,128)} %get-tuple-element.2179) | copy-start | bytes 29188 | tf_op jit(solution)/shard_map/while
  128.5 38.0 %copy-start.12 = (f32[128,152]{0,1:T(8,128)S(1)}, f32[128,152]{0,1:T(8,128)}, u32[]{:S(2)}) copy-start(f32[128,152]{0,1:T(8,128)} %custom-call.38) | copy-start | bytes 233476
  128.5 38.0 %copy-start.20 = (s32[2,24,4]{1,0,2:T(2,128)S(1)}, s32[2,24,4]{1,0,2:T(2,128)}, u32[]{:S(2)}) copy-start(s32[2,24,4]{1,0,2:T(2,128)} %reshape.1696) | copy-start | bytes 2308
  128.5 38.0 %copy-start.28 = (f32[16,152]{1,0:T(8,128)S(1)}, f32[16,152]{1,0:T(8,128)}, u32[]{:S(2)}) copy-start(f32[16,152]{1,0:T(8,128)} %custom-call.39) | copy-start | bytes 29188
  166.5 36.8 %copy-start.10 = (f32[128,152]{0,1:T(8,128)S(1)}, f32[128,152]{0,1:T(8,128)}, u32[]{:S(2)}) copy-start(f32[128,152]{0,1:T(8,128)} %custom-call.40) | copy-start | bytes 233476
  166.5 36.8 %copy-start.19 = (s32[2,24,4]{1,0,2:T(2,128)S(1)}, s32[2,24,4]{1,0,2:T(2,128)}, u32[]{:S(2)}) copy-start(s32[2,24,4]{1,0,2:T(2,128)} %reshape.1697) | copy-start | bytes 2308
  203.3 38.3 %copy-start.8 = (f32[128,152]{0,1:T(8,128)S(1)}, f32[128,152]{0,1:T(8,128)}, u32[]{:S(2)}) copy-start(f32[128,152]{0,1:T(8,128)} %custom-call.42) | copy-start | bytes 233476
  203.3 38.3 %copy-start.18 = (s32[2,24,4]{1,0,2:T(2,128)S(1)}, s32[2,24,4]{1,0,2:T(2,128)}, u32[]{:S(2)}) copy-start(s32[2,24,4]{1,0,2:T(2,128)} %reshape.1698) | copy-start | bytes 2308
  203.3 38.3 %copy-start.26 = (f32[16,152]{1,0:T(8,128)S(1)}, f32[16,152]{1,0:T(8,128)}, u32[]{:S(2)}) copy-start(f32[16,152]{1,0:T(8,128)} %custom-call.43) | copy-start | bytes 29188
  241.6 36.1 %copy-start.6 = (f32[128,152]{0,1:T(8,128)S(1)}, f32[128,152]{0,1:T(8,128)}, u32[]{:S(2)}) copy-start(f32[128,152]{0,1:T(8,128)} %custom-call.44) | copy-start | bytes 233476
  241.6 36.1 %copy-start.17 = (s32[2,24,4]{1,0,2:T(2,128)S(1)}, s32[2,24,4]{1,0,2:T(2,128)}, u32[]{:S(2)}) copy-start(s32[2,24,4]{1,0,2:T(2,128)} %reshape.1699) | copy-start | bytes 2308
  277.8 38.0 %copy-start.16 = (s32[2,24,4]{1,0,2:T(2,128)S(1)}, s32[2,24,4]{1,0,2:T(2,128)}, u32[]{:S(2)}) copy-start(s32[2,24,4]{1,0,2:T(2,128)} %reshape.1700) | copy-start | bytes 2308
  277.8 38.0 %copy-start.22 = (f32[16,152]{1,0:T(8,128)S(1)}, f32[16,152]{1,0:T(8,128)}, u32[]{:S(2)}) copy-start(f32[16,152]{1,0:T(8,128)} %custom-call.47) | copy-start | bytes 29188
  287.5 6.0 %copy-start.23 = (f32[16,152]{1,0:T(8,128)S(1)}, f32[16,152]{1,0:T(8,128)}, u32[]{:S(2)}) copy-start(f32[16,152]{1,0:T(8,128)} %get-tuple-element.2357) | copy-start | bytes 29188 | tf_op jit(solution)/shard_map/while
  305.8 6.0 %copy-start.23 = (f32[16,152]{1,0:T(8,128)S(1)}, f32[16,152]{1,0:T(8,128)}, u32[]{:S(2)}) copy-start(f32[16,152]{1,0:T(8,128)} %get-tuple-element.2357) | copy-start | bytes 29188 | tf_op jit(solution)/shard_map/while
  315.8 42.2 %copy-start.25 = (f32[16,152]{1,0:T(8,128)S(1)}, f32[16,152]{1,0:T(8,128)}, u32[]{:S(2)}) copy-start(f32[16,152]{1,0:T(8,128)} %get-tuple-element.851) | copy-start | bytes 29188
  315.8 51.5 %copy-start.33 = (s32[1,3]{1,0:T(1,128)S(1)}, s32[1,3]{1,0:T(1,128)}, u32[]{:S(2)}) copy-start(s32[1,3]{1,0:T(1,128)} %get-tuple-element.1670) | copy-start | bytes 40
  315.8 51.5 %copy-start.34 = (s32[1,3]{1,0:T(1,128)S(1)}, s32[1,3]{1,0:T(1,128)}, u32[]{:S(2)}) copy-start(s32[1,3]{1,0:T(1,128)} %get-tuple-element.1671) | copy-start | bytes 40
  315.8 78.2 %copy-start.3 = (f32[8,16,152]{2,1,0:T(8,128)S(1)}, f32[8,16,152]{2,1,0:T(8,128)}, u32[]{:S(2)}) copy-start(f32[8,16,152]{2,1,0:T(8,128)} %reshape.1702) | copy-start | bytes 233476
  315.8 78.2 %copy-start.21 = (f32[8,16]{1,0:T(8,128)S(1)}, f32[8,16]{1,0:T(8,128)}, u32[]{:S(2)}) copy-start(f32[8,16]{1,0:T(8,128)} %mul.1010) | copy-start | bytes 1540
  316.3 8.0 %copy-start.4 = (f32[128,152]{0,1:T(8,128)S(1)}, f32[128,152]{0,1:T(8,128)}, u32[]{:S(2)}) copy-start(f32[128,152]{0,1:T(8,128)} %get-tuple-element.2385) | copy-start | bytes 233476 | tf_op jit(solution)/shard_map/while
  333.9 8.0 %copy-start.4 = (f32[128,152]{0,1:T(8,128)S(1)}, f32[128,152]{0,1:T(8,128)}, u32[]{:S(2)}) copy-start(f32[128,152]{0,1:T(8,128)} %get-tuple-element.2385) | copy-start | bytes 233476 | tf_op jit(solution)/shard_map/while
  351.3 67.6 %copy-start.35 = (f32[152]{0:T(256)S(1)}, f32[152]{0:T(256)}, u32[]{:S(2)}) copy-start(f32[152]{0:T(256)} %constant.1416) | copy-start | bytes 1828
  351.3 67.6 %copy-start.36 = (f32[152]{0:T(256)S(1)}, f32[152]{0:T(256)}, u32[]{:S(2)}) copy-start(f32[152]{0:T(256)} %constant.1417) | copy-start | bytes 1828
  351.3 67.6 %copy-start.37 = (f32[152]{0:T(256)S(1)}, f32[152]{0:T(256)}, u32[]{:S(2)}) copy-start(f32[152]{0:T(256)} %constant.1418) | copy-start | bytes 1828
  359.2 59.7 %reduce-scatter.2.cloned.1.call-start = ((), (), s32[]{:S(2)}) async-start(), calls=%async_computation.1 | async-start | bytes 778240 | tf_op jit(solution)/shard_map/reduce_scatter | solution.py:218
  (18 other events, 25.7 us)
Sparse Core Ops, SparseCore 0:
  359.3 34.6 all-reduce.3
  396.6 22.2 reduce-scatter.1
where the time goes:
time: 438 us; the launch traced here: 429 us
  local copies, waits for them, and re-layouts  207 us (47%)
  matrix products  125 us (29%)
  waiting for transfers between devices  47.2 us (11%)
  other arithmetic  20.3 us (5%)
  between operations  14.3 us (3%)
  starting transfers between devices  12.1 us (3%)
    gather x32, local copies, waits for them, and re-layouts, strided_cut(): lax.dynamic_slice(stacked, (selected, starts[0], starts[1], starts[2], no...  151 us
    dot_general x16, matrix products, turn(): jnp.einsum('grk,gkl->rl', fine_sources, weights, preferred_element_type=j...  72.6 us
    dot_general x16, matrix products, turn(): jnp.einsum('grk,gkl->rl', coarse_sources, weights * 0.5, preferred_elemen...  49.8 us
    reduce_scatter x1, waiting for transfers between devices, shards(): lax.psum_scatter(jnp.stack(fine_parts), 'rep', scatter_dimension=0, tiled...  23.6 us
    psum x1, waiting for transfers between devices, shards(): coarse_check = lax.psum(jnp.stack(coarse_parts), 'rep') + coarse_inflow  23.6 us
    unnamed x78, local copies, waits for them, and re-layouts  20 us
    ppermute x2, starting transfers between devices, padded_2(): before = lax.ppermute(last, axis, up)  9.42 us
  transfers between devices with their start and end apart: 6, of which 2 were waited for; matrix products, arithmetic and copies ran while one was open for 7% of the time, Pallas kernels for 0%

commit v1 on v0

v1 whole, which is shorter than its diff:
```python
import functools

import jax
import jax.numpy as jnp
import ml_dtypes
import numpy as np
from jax import lax
from jax.experimental import pallas as pl
from jax.experimental.pallas import tpu as pltpu
from jax.sharding import PartitionSpec as P

ORDER = 6
COEFFS = 152
DEEP = 160
STRENGTH = np.float32(0.04)
MESH = pl.DeviceIdType.MESH
BF = jnp.bfloat16
F32 = jnp.float32


def surface_coordinates():
    chosen = []
    for a in range(ORDER):
        for b in range(ORDER):
            for c in range(ORDER):
                if any(q in (0, ORDER - 1) for q in (a, b, c)):
                    chosen.append((a, b, c))
    lattice = np.array(chosen, np.int32).astype(np.float32)
    return lattice * np.float32(2.0 / (ORDER - 1)) - np.float32(1.0)


def translation_table():
    u = surface_coordinates()
    near = np.float32(0.525)
    squares = []
    for axis in range(3):
        target = near * u[:, axis]
        per = []
        for o in range(-3, 4):
            source = near * u[:, axis] + np.float32(o)
            per.append((target[None, :] - source[:, None]) ** 2)
        squares.append(np.stack(per))
    table = np.zeros((7, 7, 7, DEEP, COEFFS), ml_dtypes.bfloat16)
    for z in range(7):
        for y in range(7):
            for x in range(7):
                if max(abs(z - 3), abs(y - 3), abs(x - 3)) >= 2:
                    total = squares[0][z] + squares[1][y] + squares[2][x]
                    table[z, y, x, :COEFFS] = (STRENGTH / np.sqrt(total)).astype(ml_dtypes.bfloat16)
    return table


def transfer_table():
    u = surface_coordinates()
    table = np.zeros((8, DEEP, COEFFS), ml_dtypes.bfloat16)
    for k in range(8):
        bits = (k >> 2 & 1, k >> 1 & 1, k & 1)
        total = np.zeros((COEFFS, COEFFS), np.float32)
        for axis in range(3):
            child = np.float32(bits[axis]) - np.float32(0.5) + np.float32(0.525) * u[:, axis]
            parent = np.float32(2.95) * u[:, axis]
            total = total + (child[None, :] - parent[:, None]) ** 2
        table[k, :COEFFS] = (STRENGTH / np.sqrt(total)).astype(ml_dtypes.bfloat16)
    return table


def fine_selection():
    sel = np.zeros((6, 6, 4, 4, 8, 8), np.float32)
    for j in range(6):
        for m in range(6):
            for y in range(4):
                for x in range(4):
                    yy, xx = 2 * y + j - 2, 2 * x + m - 2
                    if 0 <= yy < 8 and 0 <= xx < 8:
                        sel[j, m, y, x, yy, xx] = 1
    return sel.reshape(576, 64)


def coarse_selection():
    sel = np.zeros((6, 6, 6, 4, 2, 2, 12, 4, 4), np.float32)
    for i in range(6):
        for j in range(6):
            for m in range(6):
                for z in range(4):
                    for y in range(2):
                        for x in range(2):
                            yy, xx = 2 * y + j - 2, 2 * x + m - 2
                            if 0 <= yy < 4 and 0 <= xx < 4:
                                sel[i, j, m, z, y, x, 2 * z + i, yy, xx] = 1
    return sel.reshape(6, 576, 192)


def parent_order():
    order = np.zeros((8, 4, 4, 2, 2, 2, 4, 2, 2), np.float32)
    for z in range(8):
        for y in range(4):
            for x in range(4):
                order[z, y, x, z % 2, y % 2, x % 2, z // 2, y // 2, x // 2] = 1
    return order.reshape(128, 128)


def kernel(
    leaves, fm, fp, cm, cp, cpx, inc, c2d, sel, selc, order, w_hbm, l_hbm, out,
    ext_f, ext_c, e_f, e_c, w_v, l_v, acc, inc_x, gath, w_sem, l_sem, hs, hr, gs, gr,
):
    leaf, rep = lax.axis_index("leaf"), lax.axis_index("rep")
    bz, by = rep // 2, rep % 2
    has_low, has_high = leaf > 0, leaf < leaves - 1
    barrier = pltpu.get_barrier_semaphore()

    def greet(where):
        pl.semaphore_signal(barrier, inc=1, device_id=where, device_id_type=MESH)

    @pl.when(has_low)
    def _():
        greet({"leaf": leaf - 1})

    @pl.when(has_high)
    def _():
        greet({"leaf": leaf + 1})

    for k in range(1, 4):
        greet({"rep": (rep + k) % 4})

    def weights(c):
        return pltpu.make_async_copy(
            w_hbm.at[c // 6 + 1 - bz, c % 6 + 1 - by], w_v.at[c], w_sem.at[c]
        )

    own_l = pltpu.make_async_copy(l_hbm.at[pl.ds(2 * rep, 2)], l_v, l_sem)

    def begin(c, carry):
        weights(c).start()
        return carry

    lax.fori_loop(0, 36, begin, 0)
    own_l.start()

    def eye(size):
        return (
            lax.broadcasted_iota(jnp.int32, (size, size), 0)
            == lax.broadcasted_iota(jnp.int32, (size, size), 1)
        ).astype(F32)

    eye_f, eye_c = eye(64), eye(16)
    for z in range(16):
        layer = fm[z].astype(F32).reshape(64, COEFFS).astype(BF)
        keep = (eye_f * fp[z].astype(F32)).astype(BF)
        ext_f[z + 2] = jnp.dot(keep, layer, preferred_element_type=F32).astype(BF)
    for z in range(8):
        keep = (eye_c * cp[z].astype(F32)).astype(BF)
        ext_c[z + 2] = jnp.dot(keep, cm[z], preferred_element_type=F32).astype(BF)

    @pl.when(jnp.logical_not(has_low))
    def _():
        ext_f[0:2] = jnp.zeros((2, 64, COEFFS), BF)
        ext_c[0:2] = jnp.zeros((2, 16, COEFFS), BF)

    @pl.when(jnp.logical_not(has_high))
    def _():
        ext_f[18:20] = jnp.zeros((2, 64, COEFFS), BF)
        ext_c[10:12] = jnp.zeros((2, 16, COEFFS), BF)

    pl.semaphore_wait(barrier, 3 + has_low.astype(jnp.int32) + has_high.astype(jnp.int32))

    def halo(ref, source, target, slot, step):
        return pltpu.make_async_remote_copy(
            src_ref=ref.at[pl.ds(source, 2)],
            dst_ref=ref.at[pl.ds(target, 2)],
            send_sem=hs.at[slot],
            recv_sem=hr.at[slot],
            device_id={"leaf": leaf + step},
            device_id_type=MESH,
        )

    def down():
        return halo(ext_f, 2, 18, 0, -1), halo(ext_c, 2, 10, 1, -1)

    def up():
        return halo(ext_f, 16, 0, 2, 1), halo(ext_c, 8, 0, 3, 1)

    @pl.when(has_low)
    def _():
        for copy in down():
            copy.start()

    @pl.when(has_high)
    def _():
        for copy in up():
            copy.start()

    def widen(z, carry):
        rows = jnp.dot(sel[...], ext_f[z], preferred_element_type=F32).astype(BF)
        e_f[:, z % 2, pl.ds(pl.multiple_of(z // 2 * 16, 16), 16), :] = rows.reshape(36, 16, COEFFS)
        return carry

    lax.fori_loop(2, 18, widen, 0)
    acc[...] = jnp.zeros_like(acc)
    inc_x[...] = jnp.zeros_like(inc_x)
    inc_x[32:160] = inc[...]

    @pl.when(has_low)
    def _():
        for copy in up():
            copy.wait_recv()

    @pl.when(has_high)
    def _():
        for copy in down():
            copy.wait_recv()

    for z in (0, 1, 18, 19):
        widen(z, 0)

    coarse = ext_c[...].reshape(192, COEFFS)

    def widen_coarse(i, carry):
        rows = jnp.dot(selc[i], coarse, preferred_element_type=F32).astype(BF)
        e_c[i] = rows.reshape(36, 16, COEFFS)
        return carry

    lax.fori_loop(0, 6, widen_coarse, 0)

    def step(c, carry):
        i, j = c // 6, c % 6
        weights(c).wait()
        first = pl.multiple_of(i // 2 * 16, 16)

        def window(m):
            return jnp.concatenate(
                [e_f[j * 6 + m, i % 2, pl.ds(first, 128), :], e_c[i, j * 6 + m]], axis=0
            )

        windows = [window(m) for m in range(6)]

        def times(rows, n):
            return jnp.dot(rows, w_v[c, n, :COEFFS], preferred_element_type=F32)

        total = jnp.concatenate([times(windows[5], 6), times(windows[0], 0)], axis=0)
        for n in range(1, 6):
            total += times(jnp.concatenate([windows[n - 1], windows[n]], axis=0), n)
        acc[...] += total
        return carry

    lax.fori_loop(0, 36, step, 0)

    base = pl.multiple_of(((by + 2) * 6 + 2) * 16, 16)
    own = selc[bz + 2, pl.ds(base, 32), :].astype(F32)
    arrived = jnp.dot(own, inc_x[...], precision=lax.Precision.HIGHEST, preferred_element_type=F32)
    present = jnp.sum(own * cpx[...].astype(F32), axis=1, keepdims=True)
    check = 0.5 * jnp.concatenate([acc[128:144], acc[272:288]], axis=0) + arrived
    dense = jnp.dot(check, c2d[...], precision=lax.Precision.HIGHEST, preferred_element_type=F32)
    gath[rep] = (2.0 * dense * present).astype(BF)

    def share(k):
        return pltpu.make_async_remote_copy(
            src_ref=gath.at[rep],
            dst_ref=gath.at[rep],
            send_sem=gs.at[k - 1],
            recv_sem=gr.at[k - 1],
            device_id={"rep": (rep + k) % 4},
            device_id_type=MESH,
        )

    def receive(k):
        return pltpu.make_async_remote_copy(
            src_ref=gath.at[rep],
            dst_ref=gath.at[(rep + 4 - k) % 4],
            send_sem=gs.at[k - 1],
            recv_sem=gr.at[k - 1],
            device_id={"rep": (rep + k) % 4},
            device_id_type=MESH,
        )

    for k in range(1, 4):
        share(k).start()
    own_l.wait()
    for k in range(1, 4):
        receive(k).wait_recv()
    parents = jnp.dot(
        order[...], gath[...].reshape(128, COEFFS), preferred_element_type=F32
    ).astype(BF)
    own_f = sel[pl.ds(base, 32), :].astype(F32)
    for bx in range(2):
        down_part = jnp.dot(parents, l_v[bx, :COEFFS], preferred_element_type=F32)
        fine_check = acc[bx * 144:bx * 144 + 128] + down_part
        dense = jnp.dot(
            fine_check, c2d[...], precision=lax.Precision.HIGHEST, preferred_element_type=F32
        )
        for z in range(8):
            there = jnp.sum(
                own_f[bx * 16:bx * 16 + 16] * fp[2 * z + bz].astype(F32), axis=1, keepdims=True
            )
            out[bx, z * 16:z * 16 + 16] = dense[z * 16:z * 16 + 16] * there

    for k in range(1, 4):
        share(k).wait_send()

    @pl.when(has_low)
    def _():
        for copy in down():
            copy.wait_send()

    @pl.when(has_high)
    def _():
        for copy in up():
            copy.wait_send()


def shards(leaves, tables, fm, fp, cm, cp, inc, c2d):
    w, l, sel, selc, order = tables
    cp_row = jnp.pad(cp.reshape(1, 128), ((0, 0), (32, 32)))
    vmem = pl.BlockSpec(memory_space=pltpu.VMEM)
    hbm = pl.BlockSpec(memory_space=pl.ANY)
    dma = pltpu.SemaphoreType.DMA
    out = pl.pallas_call(
        functools.partial(kernel, leaves),
        out_shape=jax.ShapeDtypeStruct((2, 128, COEFFS), F32),
        in_specs=[vmem] * 10 + [hbm] * 2,
        out_specs=vmem,
        scratch_shapes=[
            pltpu.VMEM((20, 64, COEFFS), BF),
            pltpu.VMEM((12, 16, COEFFS), BF),
            pltpu.VMEM((36, 2, 160, COEFFS), BF),
            pltpu.VMEM((6, 36, 16, COEFFS), BF),
            pltpu.VMEM((36, 7, DEEP, COEFFS), BF),
            pltpu.VMEM((2, DEEP, COEFFS), BF),
            pltpu.VMEM((288, COEFFS), F32),
            pltpu.VMEM((192, COEFFS), F32),
            pltpu.VMEM((4, 32, COEFFS), BF),
            dma((36,)),
            dma,
            dma((4,)),
            dma((4,)),
            dma((3,)),
            dma((3,)),
        ],
        compiler_params=pltpu.CompilerParams(
            collective_id=0, has_side_effects=True, vmem_limit_bytes=52 * 2**20
        ),
    )(
        fm,
        fp.reshape(16, 1, 64),
        cm.reshape(8, 16, COEFFS),
        cp.reshape(8, 1, 16),
        cp_row,
        inc.reshape(128, COEFFS),
        c2d,
        sel,
        selc,
        order,
        w,
        l,
    )
    return out.reshape(2, 8, 4, 4, COEFFS)


def solution(mesh):
    leaves = mesh.shape["leaf"]
    tables = (
        translation_table(),
        transfer_table(),
        fine_selection().astype(ml_dtypes.bfloat16),
        coarse_selection().astype(ml_dtypes.bfloat16),
        parent_order().astype(ml_dtypes.bfloat16),
    )
    in_specs = (
        P("leaf", None, None, None),
        P("leaf", None, None),
        P("leaf", None, None, None),
        P("leaf", None, None),
        P("leaf", None, None, None),
        P(),
    )

    def body(*args):
        return shards(leaves, tuple(jnp.asarray(t) for t in tables), *args)

    out_specs = P("rep", "leaf", None, None, None)
    return jax.shard_map(body, mesh=mesh, in_specs=in_specs, out_specs=out_specs, check_vma=False)
```

time: 438 us -> 40.5 us (0.09)
  the two profiles are of different devices: /device:TPU:0 before, /device:TPU:17 now
where the time goes in v1:
time: 40.5 us; the launch traced here: 39.9 us
  Pallas kernels  29.8 us (74%)
  local copies, waits for them, and re-layouts  10.1 us (25%)
    pallas_call x1, Pallas kernels, shards(): pl.pallas_call(functools.partial(kernel, leaves), out_shape=jax.ShapeDtyp...  29.8 us
    unnamed x11, local copies, waits for them, and re-layouts  5.51 us
    reshape x1, local copies, waits for them, and re-layouts, shards(): inc.reshape(128, COEFFS)  0.95 us
    reshape x1, local copies, waits for them, and re-layouts, shards(): cm.reshape(8, 16, COEFFS)  0.89 us
    reshape x1, local copies, waits for them, and re-layouts, shards(): fp.reshape(16, 1, 64)  0.82 us

profile of v1, /device:TPU:17, one launch (start us, length us, event | category | flops | bytes accessed | tf_op | source)
XLA Modules:
  0.0 39.9 jit_solution(14484315429526621775)
XLA Ops:
  0.0 0.8 %copy.17.cp = s32[8,1,16]{2,1,0:T(1,128)S(1)} copy(s32[8,1,16]{0,2,1:T(8,128)} %bitcast.5) | data formatting | bytes 1024 | tf_op jit(solution)/shard_map/reshape | solution.py:345
  0.8 0.8 %copy.16.fp = s32[16,1,64]{2,1,0:T(1,128)S(1)} copy(s32[16,1,64]{0,2,1:T(8,128)} %bitcast.4) | data formatting | bytes 8192 | tf_op jit(solution)/shard_map/reshape | solution.py:343
  1.6 0.8 %copy.15 = s32[8,4,4]{2,1,0:T(4,128)S(1)} copy(s32[8,4,4]{0,2,1:T(4,128)} %param.14) | data formatting | bytes 1024 | tf_op args[3]
  2.4 0.1 reshape.21
  2.5 0.1 pad.4.cpx
  2.6 0.9 %reshape.19.cm = bf16[8,16,152]{2,1,0:T(8,128)(2,1)S(1)} reshape(bf16[8,4,4,152]{3,2,1,0:T(4,128)(2,1)} %param.13) | data formatting | bytes 77824 | tf_op jit(solution)/shard_map/reshape | solution.py:344
  3.5 1.0 %reshape.22.inc = f32[128,152]{1,0:T(8,128)S(1)} reshape(f32[8,4,4,152]{3,2,1,0:T(4,128)} %param.15) | data formatting | bytes 155648 | tf_op jit(solution)/shard_map/reshape | solution.py:347
  4.4 0.0 copy-start
  4.4 1.1 %copy-done = bf16[8,160,152]{2,1,0:T(8,128)(2,1)S(1)} copy-done((bf16[8,160,152]{2,1,0:T(8,128)(2,1)S(1)}, bf16[8,160,152]{2,1,0:T(8,128)(2,1)}, u32[]{:S(2)}) %copy-start) | copy-done | bytes 389144
  5.5 0.0 copy-start.1
  5.5 1.0 %copy-done.1 = bf16[16,8,8,152]{3,2,1,0:T(8,128)(2,1)S(1)} copy-done((bf16[16,8,8,152]{3,2,1,0:T(8,128)(2,1)S(1)}, bf16[16,8,8,152]{3,2,1,0:T(8,128)(2,1)}, u32[]{:S(2)}) %copy-start.1) | copy-done | bytes 311320
  6.6 0.0 copy-start.2
  6.6 0.9 %copy-done.2 = f32[152,152]{1,0:T(8,128)S(1)} copy-done((f32[152,152]{1,0:T(8,128)S(1)}, f32[152,152]{1,0:T(8,128)}, u32[]{:S(2)}) %copy-start.2) | copy-done | bytes 92440
  7.5 0.0 copy-start.3
  7.5 0.9 %copy-done.3 = bf16[576,64]{1,0:T(8,128)(2,1)S(1)} copy-done((bf16[576,64]{1,0:T(8,128)(2,1)S(1)}, bf16[576,64]{1,0:T(8,128)(2,1)}, u32[]{:S(2)}) %copy-start.3) | copy-done | bytes 73752
  8.4 0.0 copy-start.4
  8.4 0.8 %copy-done.4 = bf16[128,128]{1,0:T(8,128)(2,1)S(1)} copy-done((bf16[128,128]{1,0:T(8,128)(2,1)S(1)}, bf16[128,128]{1,0:T(8,128)(2,1)}, u32[]{:S(2)}) %copy-start.4) | copy-done | bytes 32792
  9.1 29.8 %shard_map.109 = f32[2,128,152]{2,1,0:T(8,128)S(1)} custom-call(bf16[16,8,8,152]{3,2,1,0:T(8,128)(2,1)S(1)} %copy-done.1, s32[16,1,64]{2,1,0:T(1,128)S(1)} %copy.16.fp, bf16[8,16,152]{2,1,0:T(8,128)(2,1)S(1)} %reshape.19.cm, s32[8,1,16]{2,1,0:T(1,128)S(1)} %copy.17.cp, s32[1,192]{1,0:T(1,128)S(1)} %pad.4.cpx, f32[128,152]{1,0:T(8,128)S(1)} %reshape.22.inc, ...), custom_call_target="tpu_custom_call" | custom-call | tf_op jit(solution)/shard_map/pallas_call | solution.py:316
  38.9 0.2 copy.18
  39.1 0.8 %copy.19 = f32[2,8,4,4,152]{4,3,2,1,0:T(4,128)} copy(f32[2,8,4,4,152]{4,0,3,2,1:T(2,128)S(1)} %bitcast.3) | data formatting | bytes 311296 | tf_op jit(solution)/shard_map/reshape | solution.py:355
Async XLA Ops:
  4.4 1.1 %copy-start = (bf16[8,160,152]{2,1,0:T(8,128)(2,1)S(1)}, bf16[8,160,152]{2,1,0:T(8,128)(2,1)}, u32[]{:S(2)}) copy-start(bf16[8,160,152]{2,1,0:T(8,128)(2,1)} %constant.13.clone.l_hbm) | copy-start | bytes 1167364
  5.5 1.0 %copy-start.1 = (bf16[16,8,8,152]{3,2,1,0:T(8,128)(2,1)S(1)}, bf16[16,8,8,152]{3,2,1,0:T(8,128)(2,1)}, u32[]{:S(2)}) copy-start(bf16[16,8,8,152]{3,2,1,0:T(8,128)(2,1)} %fm.1) | copy-start | bytes 933892
  6.6 0.9 %copy-start.2 = (f32[152,152]{1,0:T(8,128)S(1)}, f32[152,152]{1,0:T(8,128)}, u32[]{:S(2)}) copy-start(f32[152,152]{1,0:T(8,128)} %c2d.1) | copy-start | bytes 277252
  7.5 0.9 %copy-start.3 = (bf16[576,64]{1,0:T(8,128)(2,1)S(1)}, bf16[576,64]{1,0:T(8,128)(2,1)}, u32[]{:S(2)}) copy-start(bf16[576,64]{1,0:T(8,128)(2,1)} %constant.14.clone.sel) | copy-start | bytes 221188
  8.4 0.8 %copy-start.4 = (bf16[128,128]{1,0:T(8,128)(2,1)S(1)}, bf16[128,128]{1,0:T(8,128)(2,1)}, u32[]{:S(2)}) copy-start(bf16[128,128]{1,0:T(8,128)(2,1)} %constant.16.clone.order) | copy-start | bytes 98308

commit v2 on v1

--- a/solution.py
+++ b/solution.py
@@ -46,7 +46,7 @@
             for x in range(7):
                 if max(abs(z - 3), abs(y - 3), abs(x - 3)) >= 2:
                     total = squares[0][z] + squares[1][y] + squares[2][x]
-                    table[z, y, x, :COEFFS] = (STRENGTH / np.sqrt(total)).astype(ml_dtypes.bfloat16)
+                    table[z, y, (x + 2) % 7, :COEFFS] = (STRENGTH / np.sqrt(total)).astype(ml_dtypes.bfloat16)
     return table
 
 
@@ -100,8 +100,10 @@
 
 
 def kernel(
-    leaves, fm, fp, cm, cp, cpx, inc, c2d, sel, selc, order, w_hbm, l_hbm, out,
-    ext_f, ext_c, e_f, e_c, w_v, l_v, acc, inc_x, gath, w_sem, l_sem, hs, hr, gs, gr,
+    leaves, fm_h, fp_h, cm_h, cp_h, inc_h, c2d_h, sel_h, selc_h, order_h, back_h, w_hbm, l_hbm, out,
+    fm, fp, cm, cp, inc, c2d, sel, selc, order, back,
+    ext_f, ext_c, e_f, e_c, w_v, l_v, acc, acc_c, mask_c, nat_c, nat_m, nat_i, gath,
+    in_sem, w_sem, l_sem, hs, hr, gs, gr,
 ):
     leaf, rep = lax.axis_index("leaf"), lax.axis_index("rep")
     bz, by = rep // 2, rep % 2
@@ -122,34 +124,56 @@
     for k in range(1, 4):
         greet({"rep": (rep + k) % 4})
 
-    def weights(c):
+    inputs = [
+        pltpu.make_async_copy(source, target, in_sem.at[k])
+        for k, (source, target) in enumerate(
+            (
+                (fp_h, fp), (fm_h, fm), (cp_h, cp), (cm_h, cm), (sel_h, sel), (selc_h, selc),
+                (inc_h, inc), (c2d_h, c2d), (order_h, order), (back_h, back),
+            )
+        )
+    ]
+    for copy in inputs:
+        copy.start()
+
+    def place(a, b):
+        return (a + 1 + bz) % 6, (b + 1 + by) % 6
+
+    def weights(a, b, near):
+        i, j = place(a, b)
+        count = 4 if near else 7
+        c = a * 6 + b
         return pltpu.make_async_copy(
-            w_hbm.at[c // 6 + 1 - bz, c % 6 + 1 - by], w_v.at[c], w_sem.at[c]
+            w_hbm.at[i + 1 - bz, j + 1 - by, pl.ds(0, count)],
+            w_v.at[c, pl.ds(0, count)],
+            w_sem.at[c],
         )
 
     own_l = pltpu.make_async_copy(l_hbm.at[pl.ds(2 * rep, 2)], l_v, l_sem)
-
-    def begin(c, carry):
-        weights(c).start()
-        return carry
-
-    lax.fori_loop(0, 36, begin, 0)
+    for a in range(6):
+        for b in range(6):
+            weights(a, b, a < 3 and b < 3).start()
     own_l.start()
 
-    def eye(size):
-        return (
-            lax.broadcasted_iota(jnp.int32, (size, size), 0)
-            == lax.broadcasted_iota(jnp.int32, (size, size), 1)
-        ).astype(F32)
-
-    eye_f, eye_c = eye(64), eye(16)
-    for z in range(16):
-        layer = fm[z].astype(F32).reshape(64, COEFFS).astype(BF)
-        keep = (eye_f * fp[z].astype(F32)).astype(BF)
-        ext_f[z + 2] = jnp.dot(keep, layer, preferred_element_type=F32).astype(BF)
+    acc[...] = jnp.zeros_like(acc)
+    acc_c[...] = jnp.zeros_like(acc_c)
+    inputs[0].wait()
+    mask_f = fp[...].astype(F32).reshape(64, 16)
+    inputs[1].wait()
+    for z in (0, 1, 14, 15) + tuple(range(2, 14)):
+        layer = fm[z].astype(F32).reshape(64, COEFFS)
+        ext_f[z + 2] = (layer * mask_f[:, z:z + 1]).astype(BF)
+    inputs[2].wait()
+    inputs[3].wait()
+    for y in range(4):
+        mask_c[4 * y:4 * y + 4] = cp[y].astype(F32)
     for z in range(8):
-        keep = (eye_c * cp[z].astype(F32)).astype(BF)
-        ext_c[z + 2] = jnp.dot(keep, cm[z], preferred_element_type=F32).astype(BF)
+        for y in range(4):
+            nat_c[16 * z + 4 * y:16 * z + 4 * y + 4] = cm[z, y].astype(F32)
+    for z in range(8):
+        keep = jnp.broadcast_to(mask_c[:, z:z + 1], (16, COEFFS))
+        nat_m[16 * z:16 * z + 16] = keep.astype(BF)
+        ext_c[z + 2] = (nat_c[16 * z:16 * z + 16] * keep).astype(BF)
 
     @pl.when(jnp.logical_not(has_low))
     def _():
@@ -189,15 +213,26 @@
         for copy in up():
             copy.start()
 
-    def widen(z, carry):
+    inputs[4].wait()
+
+    def widen(z):
         rows = jnp.dot(sel[...], ext_f[z], preferred_element_type=F32).astype(BF)
-        e_f[:, z % 2, pl.ds(pl.multiple_of(z // 2 * 16, 16), 16), :] = rows.reshape(36, 16, COEFFS)
+        first = z // 2 * 16
+        if not isinstance(z, int):
+            first = pl.multiple_of(first, 16)
+        e_f[:, z % 2, pl.ds(first, 16), :] = rows.reshape(36, 16, COEFFS)
+
+    def widen_four(g, carry):
+        for q in range(4):
+            widen(2 + 4 * g + q)
         return carry
 
-    lax.fori_loop(2, 18, widen, 0)
-    acc[...] = jnp.zeros_like(acc)
-    inc_x[...] = jnp.zeros_like(inc_x)
-    inc_x[32:160] = inc[...]
+    lax.fori_loop(0, 4, widen_four, 0)
+    for k in range(5, 10):
+        inputs[k].wait()
+    for z in range(8):
+        for y in range(4):
+            nat_i[16 * z + 4 * y:16 * z + 4 * y + 4] = inc[z, y]
 
     @pl.when(has_low)
     def _():
@@ -210,45 +245,73 @@
             copy.wait_recv()
 
     for z in (0, 1, 18, 19):
-        widen(z, 0)
+        widen(z)
 
     coarse = ext_c[...].reshape(192, COEFFS)
 
-    def widen_coarse(i, carry):
-        rows = jnp.dot(selc[i], coarse, preferred_element_type=F32).astype(BF)
-        e_c[i] = rows.reshape(36, 16, COEFFS)
+    def widen_coarse(g, carry):
+        for q in range(2):
+            i = 2 * g + q
+            rows = jnp.dot(selc[i], coarse, preferred_element_type=F32).astype(BF)
+            e_c[i] = rows.reshape(36, 16, COEFFS)
         return carry
 
-    lax.fori_loop(0, 6, widen_coarse, 0)
-
-    def step(c, carry):
-        i, j = c // 6, c % 6
-        weights(c).wait()
+    lax.fori_loop(0, 3, widen_coarse, 0)
+
+    def visit(a, b, near, bx):
+        i, j = place(a, b)
+        c = a * 6 + b
         first = pl.multiple_of(i // 2 * 16, 16)
-
-        def window(m):
-            return jnp.concatenate(
-                [e_f[j * 6 + m, i % 2, pl.ds(first, 128), :], e_c[i, j * 6 + m]], axis=0
-            )
-
-        windows = [window(m) for m in range(6)]
+        if bx == 0:
+            weights(a, b, near).wait()
+
+        def fine(m):
+            return e_f[j * 6 + m, i % 2, pl.ds(first, 128), :]
+
+        def small(m):
+            return e_c[i, j * 6 + m]
 
         def times(rows, n):
-            return jnp.dot(rows, w_v[c, n, :COEFFS], preferred_element_type=F32)
-
-        total = jnp.concatenate([times(windows[5], 6), times(windows[0], 0)], axis=0)
-        for n in range(1, 6):
-            total += times(jnp.concatenate([windows[n - 1], windows[n]], axis=0), n)
-        acc[...] += total
-        return carry
-
-    lax.fori_loop(0, 36, step, 0)
-
-    base = pl.multiple_of(((by + 2) * 6 + 2) * 16, 16)
-    own = selc[bz + 2, pl.ds(base, 32), :].astype(F32)
-    arrived = jnp.dot(own, inc_x[...], precision=lax.Precision.HIGHEST, preferred_element_type=F32)
-    present = jnp.sum(own * cpx[...].astype(F32), axis=1, keepdims=True)
-    check = 0.5 * jnp.concatenate([acc[128:144], acc[272:288]], axis=0) + arrived
+            return jnp.dot(rows, w_v[c, (n + 2) % 7, :COEFFS], preferred_element_type=F32)
+
+        middle = (1, 5) if near else (1, 2, 3, 4, 5)
+        if bx == 1:
+            total = times(fine(0), 0)
+            for n in middle:
+                total += times(fine(n), n)
+            acc[1] += total
+            return
+        total = None
+        for n in middle:
+            term = times(jnp.concatenate([fine(n - 1), small(n - 1), small(n)], axis=0), n)
+            total = term if total is None else total + term
+        last = times(jnp.concatenate([fine(5), small(5)], axis=0), 6)
+        acc[0] += total[:128] + last[:128]
+        acc_c[0] += total[128:144] + last[128:]
+        acc_c[1] += total[144:] + times(small(0), 0)
+
+    def sweep(bx):
+        def some(a, carry):
+            for b in range(6):
+                visit(a, b, b < 3, bx)
+            return carry
+
+        def rest(a, carry):
+            for b in range(6):
+                visit(a, b, False, bx)
+            return carry
+
+        lax.fori_loop(0, 3, some, 0)
+        lax.fori_loop(3, 6, rest, 0)
+
+    sweep(0)
+
+    own = back[pl.ds(pl.multiple_of(rep * 32, 32), 32), :]
+    arrived = jnp.dot(
+        own.astype(F32), nat_i[...], precision=lax.Precision.HIGHEST, preferred_element_type=F32
+    )
+    present = jnp.dot(own, nat_m[...], preferred_element_type=F32)
+    check = 0.5 * jnp.concatenate([acc_c[0], acc_c[1]], axis=0) + arrived
     dense = jnp.dot(check, c2d[...], precision=lax.Precision.HIGHEST, preferred_element_type=F32)
     gath[rep] = (2.0 * dense * present).astype(BF)
 
@@ -274,24 +337,28 @@
 
     for k in range(1, 4):
         share(k).start()
+
+    sweep(1)
+
     own_l.wait()
     for k in range(1, 4):
         receive(k).wait_recv()
     parents = jnp.dot(
         order[...], gath[...].reshape(128, COEFFS), preferred_element_type=F32
     ).astype(BF)
-    own_f = sel[pl.ds(base, 32), :].astype(F32)
+    base = pl.multiple_of(((by + 2) * 6 + 2) * 16, 16)
+    there = jnp.dot(sel[pl.ds(base, 32), :], mask_f.astype(BF), preferred_element_type=F32)
     for bx in range(2):
         down_part = jnp.dot(parents, l_v[bx, :COEFFS], preferred_element_type=F32)
-        fine_check = acc[bx * 144:bx * 144 + 128] + down_part
         dense = jnp.dot(
-            fine_check, c2d[...], precision=lax.Precision.HIGHEST, preferred_element_type=F32
+            acc[bx] + down_part, c2d[...], precision=lax.Precision.HIGHEST, preferred_element_type=F32
         )
         for z in range(8):
-            there = jnp.sum(
-                own_f[bx * 16:bx * 16 + 16] * fp[2 * z + bz].astype(F32), axis=1, keepdims=True
-            )
-            out[bx, z * 16:z * 16 + 16] = dense[z * 16:z * 16 + 16] * there
+            rows = slice(bx * 16, bx * 16 + 16)
+            kept = jnp.where(bz == 1, there[rows, 2 * z + 1:2 * z + 2], there[rows, 2 * z:2 * z + 1])
+            layer = dense[z * 16:z * 16 + 16] * kept
+            for y in range(4):
+                out[bx, z, y] = layer[4 * y:4 * y + 4]
 
     for k in range(1, 4):
         share(k).wait_send()
@@ -309,25 +376,35 @@
 
 def shards(leaves, tables, fm, fp, cm, cp, inc, c2d):
     w, l, sel, selc, order = tables
-    cp_row = jnp.pad(cp.reshape(1, 128), ((0, 0), (32, 32)))
+    operands = (
+        fm, fp.transpose(1, 2, 0), cm, cp.transpose(1, 2, 0), inc, c2d,
+        sel, selc, order, order.T, w, l,
+    )
     vmem = pl.BlockSpec(memory_space=pltpu.VMEM)
-    hbm = pl.BlockSpec(memory_space=pl.ANY)
+    hbm = pl.BlockSpec(memory_space=pltpu.HBM)
     dma = pltpu.SemaphoreType.DMA
-    out = pl.pallas_call(
+    operands = tuple(jnp.asarray(t) for t in operands)
+    return pl.pallas_call(
         functools.partial(kernel, leaves),
-        out_shape=jax.ShapeDtypeStruct((2, 128, COEFFS), F32),
-        in_specs=[vmem] * 10 + [hbm] * 2,
+        out_shape=jax.ShapeDtypeStruct((2, 8, 4, 4, COEFFS), F32),
+        in_specs=[hbm] * 12,
         out_specs=vmem,
-        scratch_shapes=[
+        scratch_shapes=[pltpu.VMEM(t.shape, t.dtype) for t in operands[:10]]
+        + [
             pltpu.VMEM((20, 64, COEFFS), BF),
             pltpu.VMEM((12, 16, COEFFS), BF),
             pltpu.VMEM((36, 2, 160, COEFFS), BF),
             pltpu.VMEM((6, 36, 16, COEFFS), BF),
             pltpu.VMEM((36, 7, DEEP, COEFFS), BF),
             pltpu.VMEM((2, DEEP, COEFFS), BF),
-            pltpu.VMEM((288, COEFFS), F32),
-            pltpu.VMEM((192, COEFFS), F32),
+            pltpu.VMEM((2, 128, COEFFS), F32),
+            pltpu.VMEM((2, 16, COEFFS), F32),
+            pltpu.VMEM((16, 8), F32),
+            pltpu.VMEM((128, COEFFS), F32),
+            pltpu.VMEM((128, COEFFS), BF),
+            pltpu.VMEM((128, COEFFS), F32),
             pltpu.VMEM((4, 32, COEFFS), BF),
+            dma((10,)),
             dma((36,)),
             dma,
             dma((4,)),
@@ -338,21 +415,7 @@
         compiler_params=pltpu.CompilerParams(
             collective_id=0, has_side_effects=True, vmem_limit_bytes=52 * 2**20
         ),
-    )(
-        fm,
-        fp.reshape(16, 1, 64),
-        cm.reshape(8, 16, COEFFS),
-        cp.reshape(8, 1, 16),
-        cp_row,
-        inc.reshape(128, COEFFS),
-        c2d,
-        sel,
-        selc,
-        order,
-        w,
-        l,
-    )
-    return out.reshape(2, 8, 4, 4, COEFFS)
+    )(*operands)
 
 
 def solution(mesh):
@@ -374,7 +437,7 @@
     )
 
     def body(*args):
-        return shards(leaves, tuple(jnp.asarray(t) for t in tables), *args)
+        return shards(leaves, tables, *args)
 
     out_specs = P("rep", "leaf", None, None, None)
     return jax.shard_map(body, mesh=mesh, in_specs=in_specs, out_specs=out_specs, check_vma=False)

time: 40.5 us -> 36.7 us (0.906)
  Pallas kernels: 29.8 us -> 27.9 us
  local copies, waits for them, and re-layouts: 10.1 us -> 8.28 us
    reshape x6 -> x0, local copies, waits for them, and re-layouts: 4.3 us -> none  [the longest x1 0.95 us: shards(): inc.reshape(128, COEFFS)]
    unnamed x11 -> x19, local copies, waits for them, and re-layouts: 5.51 us -> 8.28 us
    pallas_call x1, Pallas kernels: 29.8 us -> 27.9 us  [shards(): pl.pallas_call(functools.partial(kernel, leaves), out_shape=jax.ShapeDtyp...]
where the time goes in v2:
time: 36.7 us; the launch traced here: 36.2 us
  Pallas kernels  27.9 us (76%)
  local copies, waits for them, and re-layouts  8.28 us (23%)
    pallas_call x1, Pallas kernels, shards(): pl.pallas_call(functools.partial(kernel, leaves), out_shape=jax.ShapeDtyp...  27.9 us
    unnamed x19, local copies, waits for them, and re-layouts  8.28 us

profile of v2, /device:TPU:17, one launch (start us, length us, event | category | flops | bytes accessed | tf_op | source)
XLA Modules:
  0.0 36.2 jit_solution(18020159459404770929)
XLA Ops:
  0.0 0.0 copy-start
  0.0 1.0 %copy-done = bf16[16,8,8,152]{3,2,1,0:T(8,128)(2,1)S(1)} copy-done((bf16[16,8,8,152]{3,2,1,0:T(8,128)(2,1)S(1)}, bf16[16,8,8,152]{3,2,1,0:T(8,128)(2,1)}, u32[]{:S(2)}) %copy-start) | copy-done | bytes 311320
  1.0 0.0 copy-start.1
  1.0 0.9 %copy-done.1 = f32[152,152]{1,0:T(8,128)S(1)} copy-done((f32[152,152]{1,0:T(8,128)S(1)}, f32[152,152]{1,0:T(8,128)}, u32[]{:S(2)}) %copy-start.1) | copy-done | bytes 92440
  2.0 0.0 copy-start.2
  2.0 0.9 %copy-done.2 = bf16[576,64]{1,0:T(8,128)(2,1)S(1)} copy-done((bf16[576,64]{1,0:T(8,128)(2,1)S(1)}, bf16[576,64]{1,0:T(8,128)(2,1)}, u32[]{:S(2)}) %copy-start.2) | copy-done | bytes 73752
  2.9 0.0 copy-start.3
  2.9 0.9 %copy-done.3 = f32[8,4,4,152]{3,2,1,0:T(4,128)S(1)} copy-done((f32[8,4,4,152]{3,2,1,0:T(4,128)S(1)}, f32[8,4,4,152]{3,2,1,0:T(4,128)}, u32[]{:S(2)}) %copy-start.3) | copy-done | bytes 77848
  3.8 0.0 copy-start.4
  3.8 0.8 %copy-done.4 = bf16[8,4,4,152]{3,2,1,0:T(4,128)(2,1)S(1)} copy-done((bf16[8,4,4,152]{3,2,1,0:T(4,128)(2,1)S(1)}, bf16[8,4,4,152]{3,2,1,0:T(4,128)(2,1)}, u32[]{:S(2)}) %copy-start.4) | copy-done | bytes 38936
  4.6 0.0 copy-start.5
  4.6 0.8 %copy-done.5 = s32[16,8,8]{0,2,1:T(8,128)S(1)} copy-done((s32[16,8,8]{0,2,1:T(8,128)S(1)}, s32[16,8,8]{0,2,1:T(8,128)}, u32[]{:S(2)}) %copy-start.5) | copy-done | bytes 4120
  5.4 0.0 copy-start.6
  5.4 0.8 %copy-done.6 = bf16[128,128]{1,0:T(8,128)(2,1)S(1)} copy-done((bf16[128,128]{1,0:T(8,128)(2,1)S(1)}, bf16[128,128]{1,0:T(8,128)(2,1)}, u32[]{:S(2)}) %copy-start.6) | copy-done | bytes 32792
  6.1 0.0 copy-start.7
  6.1 0.8 %copy-done.7 = bf16[128,128]{1,0:T(8,128)(2,1)S(1)} copy-done((bf16[128,128]{1,0:T(8,128)(2,1)S(1)}, bf16[128,128]{1,0:T(8,128)(2,1)}, u32[]{:S(2)}) %copy-start.7) | copy-done | bytes 32792
  6.9 0.0 copy-start.8
  6.9 0.7 %copy-done.8 = s32[8,4,4]{0,2,1:T(4,128)S(1)} copy-done((s32[8,4,4]{0,2,1:T(4,128)S(1)}, s32[8,4,4]{0,2,1:T(4,128)}, u32[]{:S(2)}) %copy-start.8) | copy-done | bytes 536
  7.6 27.9 %shard_map.118 = f32[2,8,4,4,152]{4,3,2,1,0:T(4,128)S(1)} custom-call(bf16[16,8,8,152]{3,2,1,0:T(8,128)(2,1)S(1)} %copy-done, s32[8,8,16]{2,1,0:T(8,128)S(1)} %bitcast.2, bf16[8,4,4,152]{3,2,1,0:T(4,128)(2,1)S(1)} %copy-done.4, s32[4,4,8]{2,1,0:T(4,128)S(1)} %bitcast.3, f32[8,4,4,152]{3,2,1,0:T(4,128)S(1)} %copy-done.3, f32[152,152]{1,0:T(8,128)S(1)} %copy-done.1, ...), custom_call_target="tpu_custom_call" | custom-call | tf_op jit(solution)/shard_map/pallas_call | solution.py:387
  35.5 0.7 %copy.14 = f32[2,8,4,4,152]{4,3,2,1,0:T(4,128)} copy(f32[2,8,4,4,152]{4,3,2,1,0:T(4,128)S(1)} %shard_map.118) | data formatting | bytes 311296
Async XLA Ops:
  0.0 1.0 %copy-start = (bf16[16,8,8,152]{3,2,1,0:T(8,128)(2,1)S(1)}, bf16[16,8,8,152]{3,2,1,0:T(8,128)(2,1)}, u32[]{:S(2)}) copy-start(bf16[16,8,8,152]{3,2,1,0:T(8,128)(2,1)} %fm_h.1) | copy-start | bytes 933892
  1.0 0.9 %copy-start.1 = (f32[152,152]{1,0:T(8,128)S(1)}, f32[152,152]{1,0:T(8,128)}, u32[]{:S(2)}) copy-start(f32[152,152]{1,0:T(8,128)} %c2d_h.1) | copy-start | bytes 277252
  2.0 0.9 %copy-start.2 = (bf16[576,64]{1,0:T(8,128)(2,1)S(1)}, bf16[576,64]{1,0:T(8,128)(2,1)}, u32[]{:S(2)}) copy-start(bf16[576,64]{1,0:T(8,128)(2,1)} %constant.12.clone.sel_h) | copy-start | bytes 221188
  2.9 0.9 %copy-start.3 = (f32[8,4,4,152]{3,2,1,0:T(4,128)S(1)}, f32[8,4,4,152]{3,2,1,0:T(4,128)}, u32[]{:S(2)}) copy-start(f32[8,4,4,152]{3,2,1,0:T(4,128)} %inc_h.1) | copy-start | bytes 233476
  3.8 0.8 %copy-start.4 = (bf16[8,4,4,152]{3,2,1,0:T(4,128)(2,1)S(1)}, bf16[8,4,4,152]{3,2,1,0:T(4,128)(2,1)}, u32[]{:S(2)}) copy-start(bf16[8,4,4,152]{3,2,1,0:T(4,128)(2,1)} %cm_h.1) | copy-start | bytes 116740
  4.6 0.8 %copy-start.5 = (s32[16,8,8]{0,2,1:T(8,128)S(1)}, s32[16,8,8]{0,2,1:T(8,128)}, u32[]{:S(2)}) copy-start(s32[16,8,8]{0,2,1:T(8,128)} %param.13) | copy-start | bytes 12292
  5.4 0.8 %copy-start.6 = (bf16[128,128]{1,0:T(8,128)(2,1)S(1)}, bf16[128,128]{1,0:T(8,128)(2,1)}, u32[]{:S(2)}) copy-start(bf16[128,128]{1,0:T(8,128)(2,1)} %constant.15.clone.back_h) | copy-start | bytes 98308
  6.1 0.8 %copy-start.7 = (bf16[128,128]{1,0:T(8,128)(2,1)S(1)}, bf16[128,128]{1,0:T(8,128)(2,1)}, u32[]{:S(2)}) copy-start(bf16[128,128]{1,0:T(8,128)(2,1)} %constant.14.clone.order_h) | copy-start | bytes 98308
  6.9 0.7 %copy-start.8 = (s32[8,4,4]{0,2,1:T(4,128)S(1)}, s32[8,4,4]{0,2,1:T(4,128)}, u32[]{:S(2)}) copy-start(s32[8,4,4]{0,2,1:T(4,128)} %param.15) | copy-start | bytes 1540

commit v3 on v2

--- a/solution.py
+++ b/solution.py
@@ -227,7 +227,7 @@
             widen(2 + 4 * g + q)
         return carry
 
-    lax.fori_loop(0, 4, widen_four, 0)
+    lax.fori_loop(0, 4, widen_four, 0, unroll=4)
     for k in range(5, 10):
         inputs[k].wait()
     for z in range(8):
@@ -256,14 +256,12 @@
             e_c[i] = rows.reshape(36, 16, COEFFS)
         return carry
 
-    lax.fori_loop(0, 3, widen_coarse, 0)
+    lax.fori_loop(0, 3, widen_coarse, 0, unroll=3)
 
     def visit(a, b, near, bx):
         i, j = place(a, b)
         c = a * 6 + b
         first = pl.multiple_of(i // 2 * 16, 16)
-        if bx == 0:
-            weights(a, b, near).wait()
 
         def fine(m):
             return e_f[j * 6 + m, i % 2, pl.ds(first, 128), :]
@@ -291,18 +289,25 @@
         acc_c[1] += total[144:] + times(small(0), 0)
 
     def sweep(bx):
+        def ready(a, close):
+            if bx == 0:
+                for b in range(6):
+                    weights(a, b, close and b < 3).wait()
+
         def some(a, carry):
+            ready(a, True)
             for b in range(6):
                 visit(a, b, b < 3, bx)
             return carry
 
         def rest(a, carry):
+            ready(a, False)
             for b in range(6):
                 visit(a, b, False, bx)
             return carry
 
-        lax.fori_loop(0, 3, some, 0)
-        lax.fori_loop(3, 6, rest, 0)
+        lax.fori_loop(0, 3, some, 0, unroll=3)
+        lax.fori_loop(3, 6, rest, 0, unroll=3)
 
     sweep(0)
 
@@ -413,7 +418,7 @@
             dma((3,)),
         ],
         compiler_params=pltpu.CompilerParams(
-            collective_id=0, has_side_effects=True, vmem_limit_bytes=52 * 2**20
+            collective_id=0, has_side_effects=True, vmem_limit_bytes=63 * 2**20
         ),
     )(*operands)
 

time: 36.7 us -> 25.8 us (0.70)
  local copies, waits for them, and re-layouts: 8.28 us -> 1.67 us
  Pallas kernels: 27.9 us -> 23.9 us
    unnamed x19 -> x1, local copies, waits for them, and re-layouts: 8.28 us -> 1.67 us
    pallas_call x1, Pallas kernels: 27.9 us -> 23.9 us  [shards(): pl.pallas_call(functools.partial(kernel, leaves), out_shape=jax.ShapeDtyp...]
where the time goes in v3:
time: 25.8 us; the launch traced here: 25.6 us
  Pallas kernels  23.9 us (93%)
  local copies, waits for them, and re-layouts  1.67 us (6%)
    pallas_call x1, Pallas kernels, shards(): pl.pallas_call(functools.partial(kernel, leaves), out_shape=jax.ShapeDtyp...  23.9 us
    unnamed x1, local copies, waits for them, and re-layouts  1.67 us

profile of v3, /device:TPU:17, one launch (start us, length us, event | category | flops | bytes accessed | tf_op | source)
XLA Modules:
  0.0 25.6 jit_solution(7374789489892318411)
XLA Ops:
  0.0 23.9 %shard_map.118 = f32[2,8,4,4,152]{4,3,2,1,0:T(4,128)} custom-call(bf16[16,8,8,152]{3,2,1,0:T(8,128)(2,1)} %fm_h.1, s32[8,8,16]{2,1,0:T(8,128)} %bitcast.2, bf16[8,4,4,152]{3,2,1,0:T(4,128)(2,1)} %cm_h.1, s32[4,4,8]{2,1,0:T(4,128)} %bitcast.3, f32[8,4,4,152]{3,2,1,0:T(4,128)} %inc_h.1, f32[152,152]{1,0:T(8,128)} %c2d_h.1, ...), custom_call_target="tpu_custom_call" | custom-call | tf_op jit(solution)/shard_map/pallas_call | solution.py:392
  23.9 1.7 %copy.14 = f32[2,8,4,4,152]{4,3,2,1,0:T(4,128)} copy(f32[2,8,4,4,152]{4,3,2,1,0:T(4,128)} %shard_map.118) | data formatting | bytes 311296

commit v4 on v3

--- a/solution.py
+++ b/solution.py
@@ -150,10 +150,9 @@
         )
 
     own_l = pltpu.make_async_copy(l_hbm.at[pl.ds(2 * rep, 2)], l_v, l_sem)
-    for a in range(6):
+    for a in range(2):
         for b in range(6):
             weights(a, b, a < 3 and b < 3).start()
-    own_l.start()
 
     acc[...] = jnp.zeros_like(acc)
     acc_c[...] = jnp.zeros_like(acc_c)
@@ -213,6 +212,10 @@
         for copy in up():
             copy.start()
 
+    for a in range(2, 6):
+        for b in range(6):
+            weights(a, b, a < 3 and b < 3).start()
+    own_l.start()
     inputs[4].wait()
 
     def widen(z):

time: 25.8 us -> 22 us (0.85)
  Pallas kernels: 23.9 us -> 20.2 us
    pallas_call x1, Pallas kernels: 23.9 us -> 20.2 us  [shards(): pl.pallas_call(functools.partial(kernel, leaves), out_shape=jax.ShapeDtyp...]
where the time goes in v4:
time: 22 us; the launch traced here: 21.9 us
  Pallas kernels  20.2 us (92%)
  local copies, waits for them, and re-layouts  1.67 us (8%)
    pallas_call x1, Pallas kernels, shards(): pl.pallas_call(functools.partial(kernel, leaves), out_shape=jax.ShapeDtyp...  20.2 us
    unnamed x1, local copies, waits for them, and re-layouts  1.67 us

profile of v4, /device:TPU:17, one launch (start us, length us, event | category | flops | bytes accessed | tf_op | source)
XLA Modules:
  0.0 21.9 jit_solution(1481386494592511444)
XLA Ops:
  0.0 20.2 %shard_map.118 = f32[2,8,4,4,152]{4,3,2,1,0:T(4,128)} custom-call(bf16[16,8,8,152]{3,2,1,0:T(8,128)(2,1)} %fm_h.1, s32[8,8,16]{2,1,0:T(8,128)} %bitcast.2, bf16[8,4,4,152]{3,2,1,0:T(4,128)(2,1)} %cm_h.1, s32[4,4,8]{2,1,0:T(4,128)} %bitcast.3, f32[8,4,4,152]{3,2,1,0:T(4,128)} %inc_h.1, f32[152,152]{1,0:T(8,128)} %c2d_h.1, ...), custom_call_target="tpu_custom_call" | custom-call | tf_op jit(solution)/shard_map/pallas_call | solution.py:395
  20.2 1.7 %copy.14 = f32[2,8,4,4,152]{4,3,2,1,0:T(4,128)} copy(f32[2,8,4,4,152]{4,3,2,1,0:T(4,128)} %shard_map.118) | data formatting | bytes 311296
